TPU v7x, 128 devices: a whole 4x4x4 slice. The times are simulated.
128 devices in a mesh: dp: 16 (over y, x), tensor: 8 (over z, core).
Axes of the slice: x: 4, y: 4, z: 4, core: 2. Of those that a mesh axis runs over, the one named last changes fastest.
Arguments:
- hidden_input: bfloat16 [16384, 8192], P('dp'), may hold values from -6 to 6
- key_value_gradient: bfloat16 [2, 16384, 1024], P(None, 'dp', 'tensor'), may hold values from -6 to 6
- key_value_weight: bfloat16 [2, 8192, 1024], P(None, None, 'tensor'), may hold values from -0.0625 to 0.0625
- down_adapters: bfloat16 [128, 32, 8192], P(None, None, 'tensor'), may hold values from -0.0625 to 0.0625
- up_adapters: bfloat16 [128, 2, 16, 1024], P(None, None, None, 'tensor'), may hold values from -0.1875 to 0.1875
- adapter_inner_saved: bfloat16 [32, 16384], P(None, 'dp'), may hold values from -2 to 2
- block_owner_tenant: int32 [128], P('dp'), may hold values from 0 to 127
- live_block_counts: int32 [16], P('dp'), may hold values from 1 to 8, as said below
- tenant_position: int32 [128], replicated, may hold values from 0 to 127, each once
Outputs:
- hidden_gradient: bfloat16 [16384, 8192], P('dp', 'tensor')
- grad_a: float32 [128, 32, 8192], P('dp', None, 'tensor')
- grad_b: float32 [128, 2, 16, 1024], P('dp', None, None, 'tensor')
Inputs may be any that keep to these rules, and one draw needn't show every extreme that they name: `live_block_counts`: some index of dp has all 8 block slots live.
All inputs are finite; a program needn't handle non-finite values.
Results may differ from a plain program's by a relative error of at most 0.022.
Values may be sent and summed in bfloat16 or wider, within the bound.
A program may use at most 192 MiB of HBM per device.

v0:
```python
import jax
import jax.numpy as jnp
from jax import lax
from jax.sharding import PartitionSpec as P


def per_device(
    hidden_input,
    key_value_gradient,
    key_value_weight,
    down_adapters,
    up_adapters,
    adapter_inner_saved,
    block_owner_tenant,
    live_block_counts,
    tenant_position,
):
    tok_rows = hidden_input.shape[0]
    block_list = block_owner_tenant.shape[0]
    block_length = tok_rows // block_list
    head_cols = key_value_gradient.shape[2]
    width_cols = down_adapters.shape[2]
    tenants = tenant_position.shape[0]
    rank_row_slice = down_adapters.shape[1]
    live_blk = jnp.arange(block_list, dtype=jnp.int32) < live_block_counts[0]
    live_tok = jnp.broadcast_to(live_blk[:, None], (block_list, block_length)).reshape(tok_rows)
    grad = key_value_gradient * live_tok.astype(jnp.bfloat16)[None, :, None]
    picked = block_owner_tenant[:, None] == jnp.arange(tenants, dtype=jnp.int32)[None, :]
    slot_blk = jnp.sum(jnp.where(picked, tenant_position[None, :], 0), axis=1)
    b_sel = jnp.take(up_adapters, block_owner_tenant, axis=0)
    g_blk = grad.reshape(2, block_list, block_length, head_cols)
    inner_part = jnp.einsum("cbij,bcrj->bicr", g_blk, b_sel, preferred_element_type=jnp.float32)
    inner = lax.psum(inner_part.reshape(tok_rows, rank_row_slice).astype(jnp.bfloat16), "tensor")
    inner_block = inner.reshape(block_list, block_length, rank_row_slice)
    selected_down = jnp.take(down_adapters, block_owner_tenant, axis=0)
    adapter_input_gradient = jnp.einsum(
        "hxr,hrg->hxg", inner_block, selected_down, preferred_element_type=jnp.float32
    ).reshape(tok_rows, width_cols)
    partial_value = jnp.einsum(
        "cnj,cdj->nd", grad, key_value_weight, preferred_element_type=jnp.float32
    )
    base_offset = lax.psum_scatter(
        partial_value.astype(jnp.bfloat16), "tensor", scatter_dimension=1, tiled=True
    ).astype(jnp.float32)
    hidden_gradient = (base_offset + 2.0 * adapter_input_gradient).astype(jnp.bfloat16)
    x_cols = lax.dynamic_slice_in_dim(
        hidden_input, lax.axis_index("tensor") * width_cols, width_cols, 1
    )
    per_a = jnp.einsum(
        "bic,bid->bcd",
        inner_block,
        x_cols.reshape(block_list, block_length, width_cols),
        preferred_element_type=jnp.float32,
    )
    hidden_block = adapter_inner_saved.reshape(2, rank_row_slice // 2, block_list, block_length)
    per_b = jnp.einsum("crbi,cbij->bcrj", hidden_block, g_blk, preferred_element_type=jnp.float32)
    per_block = 2.0 * jnp.concatenate(
        [per_a, per_b.reshape(block_list, rank_row_slice, head_cols)], axis=2
    )
    owned_rows = tenants // lax.axis_size("dp")
    onehot = (
        slot_blk[None, :] == jnp.arange(owned_rows * lax.axis_size("dp"), dtype=jnp.int32)[:, None]
    ).astype(jnp.float32)
    owned = lax.psum_scatter(
        jnp.einsum("sb,bcd->scd", onehot, per_block, precision=lax.Precision.HIGHEST).astype(
            jnp.bfloat16
        ),
        "dp",
        scatter_dimension=0,
        tiled=True,
    ).astype(jnp.float32)
    grad_a = owned[:, :, :width_cols]
    grad_b = owned[:, :, width_cols:].reshape(owned_rows, 2, rank_row_slice // 2, head_cols)
    return (hidden_gradient, grad_a, grad_b)


def solution(mesh):
    return jax.shard_map(
        per_device,
        mesh=mesh,
        in_specs=(
            P("dp", None),
            P(None, "dp", "tensor"),
            P(None, None, "tensor"),
            P(None, None, "tensor"),
            P(None, None, None, "tensor"),
            P(None, "dp"),
            P("dp"),
            P("dp"),
            P(),
        ),
        out_specs=(P("dp", "tensor"), P("dp", None, "tensor"), P("dp", None, None, "tensor")),
        check_vma=False,
    )
```

profile of v0, /device:TPU:1, one launch (start us, length us, event | category | flops | bytes accessed | tf_op | source)
XLA Modules:
  0.0 339.3 jit_solution(14579576244899069147)
XLA Ops:
  7.2 0.0 copy-start
  7.2 0.0 copy-start.5
  7.2 0.0 copy-start.6
  7.2 0.0 all-reduce.4.cloned.1.call-start
  7.2 0.7 compare_select_fusion
  8.0 0.7 compare_and_fusion
  9.3 0.1 broadcast_bitcast_fusion
  9.4 1.2 broadcast_multiply_fusion
  10.6 0.0 copy-done
  10.6 0.0 copy-start.2
  10.7 0.6 gather_fusion
  11.2 1.1 convolution_convert_fusion.1
  12.3 0.0 all-reduce.4.cloned.1.call-update
  12.3 0.0 all-reduce.6.cloned.1.call-start
  12.4 0.9 copy.32
  13.2 0.2 fusion.4
  13.5 0.0 copy-done.2
  13.5 1.8 constant_dynamic-slice_fusion
  15.2 0.0 copy-done.5
  15.2 0.0 copy-done.6
  15.3 0.2 select_reduce_fusion
  15.4 57.1 %all-reduce.4.cloned.1.call-done = bf16[8,128,32]{1,2,0:T(8,128)(2,1)} async-done(((bf16[8,128,32]{1,2,0:T(8,128)(2,1)}), bf16[8,128,32]{1,2,0:T(8,128)(2,1)}) %all-reduce.4.cloned.1.call-update) | async-done | bytes 65552 | tf_op jit(solution)/shard_map/psum | solution.py:33
  72.5 1.2 fusion.17
  73.8 0.1 maximum_multiply_fusion
  73.9 9.9 %convolution_convert_fusion = bf16[128,32,1152]{2,0,1:T(8,128)(2,1)} fusion(f32[8,32,1152]{2,1,0:T(8,128)S(1)} %maximum_multiply_fusion, s32[8]{0:T(128)S(1)} %select_reduce_fusion), kind=kOutput, calls=%fused_computation.3 | convolution fusion | flops 457704448 | bytes 10616864 | tf_op jit(solution)/shard_map/sb,bcd->scd/dot_general | solution.py:65
  83.8 0.0 copy-start.3
  83.8 0.0 all-reduce.6.cloned.1.call-update
  83.8 0.0 reduce-scatter.3.cloned.1.call-start
  83.8 1.0 copy-done.3
  84.8 10.8 %bitcast_convert_fusion = bf16[1024,8192]{1,0:T(8,128)(2,1)} fusion(bf16[2,1024,128]{2,1,0:T(8,128)(2,1)S(1)} %copy-done.3, bf16[2,8192,128]{2,1,0:T(8,128)(2,1)} %param.11), kind=kOutput, calls=%fused_computation.2 | convolution fusion | flops 4303355904 | bytes 21495808 | tf_op jit(solution)/shard_map/cnj,cdj->nd/dot_general | solution.py:39
  95.6 0.0 copy-start.7
  95.6 0.0 copy-start.4
  95.6 0.0 reduce-scatter.3.cloned.1.call-update
  95.6 4.0 %gather_fusion.1 = bf16[8,32,1024]{2,1,0:T(8,128)(2,1)S(1)} fusion(bf16[128,32,1024]{2,1,0:T(8,128)(2,1)} %param.12, s32[1024]{0:T(1024)S(1)} %pad_clamp_fusion), kind=kCustom, calls=%fused_computation.1 | custom fusion | bytes 1048608 | tf_op jit(solution)/shard_map/jit(_take)/gather | solution.py:35
  99.6 0.0 copy-done.7
  99.6 0.6 dynamic-slice
  100.9 0.0 copy-done.4
  100.9 2.7 convolution_multiply_fusion
  103.6 130.9 %all-reduce.6.cloned.1.call-done = bf16[128,32,1152]{2,0,1:T(8,128)(2,1)} async-done(((bf16[128,32,1152]{2,0,1:T(8,128)(2,1)}), bf16[128,32,1152]{2,0,1:T(8,128)(2,1)}) %all-reduce.6.cloned.1.call-update) | async-done | bytes 9437200
  234.5 1.1 dynamic-slice_convert_fusion
  235.6 0.1 slice.12
  235.8 1.6 copy.28
  237.3 0.0 copy-start.1
  237.3 0.7 copy.29
  238.0 89.8 %reduce-scatter.3.cloned.1.call-done = bf16[1024,1024]{1,0:T(8,128)(2,1)} async-done(((bf16[1024,8192]{1,0:T(8,128)(2,1)}), bf16[1024,1024]{1,0:T(8,128)(2,1)}) %reduce-scatter.3.cloned.1.call-update) | async-done | bytes 2097168 | tf_op jit(solution)/shard_map/reduce_scatter | solution.py:42
  327.8 5.0 %fusion = bf16[1024,1024]{1,0:T(8,128)(2,1)} fusion(f32[8,128,1024]{2,1,0:T(8,128)} %convolution_multiply_fusion, bf16[1024,1024]{1,0:T(8,128)(2,1)} %reduce-scatter.3.cloned.1.call-done), kind=kLoop, calls=%fused_computation.5 | loop fusion | flops 3145728 | bytes 8388608 | tf_op jit(solution)/shard_map/convert_element_type | solution.py:45
  332.8 0.0 copy-done.1
  (3 shorter events, 0.0 us)
Async XLA Ops:
  7.2 3.5 %copy-start = (bf16[128,2,16,128]{3,2,1,0:T(8,128)(2,1)S(1)}, bf16[128,2,16,128]{3,2,1,0:T(8,128)(2,1)}, u32[]{:S(2)}) copy-start(bf16[128,2,16,128]{3,2,1,0:T(8,128)(2,1)} %param.13) | copy-start | bytes 3145732
  7.2 8.1 %copy-start.5 = (s32[8]{0:T(128)S(1)}, s32[8]{0:T(128)}, u32[]{:S(2)}) copy-start(s32[8]{0:T(128)} %param.15) | copy-start | bytes 100
  7.2 8.1 %copy-start.6 = (s32[128]{0:T(128)S(1)}, s32[128]{0:T(128)}, u32[]{:S(2)}) copy-start(s32[128]{0:T(128)} %param.17) | copy-start | bytes 1540
  7.2 65.3 %all-reduce.4.cloned.1.call-start = ((), (), s32[]{:S(2)}) async-start(), calls=%async_computation.2 | async-start | bytes 131072 | tf_op jit(solution)/shard_map/psum | solution.py:33
  10.6 2.8 copy-start.2
  12.3 222.2 %all-reduce.6.cloned.1.call-start = ((), (), s32[]{:S(2)}) async-start(), calls=%async_computation.3 | async-start | bytes 18874368
  83.8 1.0 copy-start.3
  83.8 244.0 %reduce-scatter.3.cloned.1.call-start = ((), (), s32[]{:S(2)}) async-start(), calls=%async_computation.1 | async-start | bytes 18874368 | tf_op jit(solution)/shard_map/reduce_scatter | solution.py:42
  95.6 4.0 %copy-start.7 = (u32[128]{0:T(128)S(1)}, u32[128]{0:T(128)}, u32[]{:S(2)}) copy-start(u32[128]{0:T(128)} %constant.44) | copy-start | bytes 1540
  95.6 5.3 %copy-start.4 = (bf16[8,128,32]{1,2,0:T(8,128)(2,1)S(1)}, bf16[8,128,32]{1,2,0:T(8,128)(2,1)}, u32[]{:S(2)}) copy-start(bf16[8,128,32]{1,2,0:T(8,128)(2,1)} %all-reduce.4.cloned.1.call-done) | copy-start | bytes 196612
  237.3 95.4 %copy-start.1 = (bf16[128,2,16,128]{3,2,1,0:T(8,128)(2,1)S(1)}, bf16[128,2,16,128]{3,2,1,0:T(8,128)(2,1)}, u32[]{:S(2)}) copy-start(bf16[128,2,16,128]{3,2,1,0:T(8,128)(2,1)} %param.13) | copy-start | bytes 3145732
Sparse Core Ops, SparseCore 0:
  12.4 60.0 all-reduce.3
  83.9 150.5 all-reduce.5
  236.9 90.8 reduce-scatter.2
where the time goes:
time: 340 us; the launch traced here: 339 us
  waiting for transfers between devices  278 us (82%)
  matrix products  25.9 us (8%)
  between operations  15.2 us (4%)
  local copies, waits for them, and re-layouts  11.2 us (3%)
  other arithmetic  9.03 us (3%)
    unnamed x4, waiting for transfers between devices  131 us
    reduce_scatter x1, waiting for transfers between devices, per_device(): lax.psum_scatter(partial_value.astype(jnp.bfloat16), 'tensor', scatter_di...  89.8 us
    psum x1, waiting for transfers between devices, per_device(): lax.psum(inner_part.reshape(tok_rows, rank_row_slice).astype(jnp.bfloat16...  57.1 us
    dot_general x1, matrix products, per_device(): jnp.einsum('cnj,cdj->nd', grad, key_value_weight, preferred_element_type=...  10.8 us
    dot_general x1, matrix products, per_device(): jnp.einsum('sb,bcd->scd', onehot, per_block, precision=lax.Precision.HIGH...  9.89 us
  transfers between devices with their start and end apart: 3, of which 3 were waited for; matrix products, arithmetic and copies ran while one was open for 7% of the time, Pallas kernels for 0%

commit v1 on v0

--- a/solution.py
+++ b/solution.py
@@ -30,7 +30,10 @@
     b_sel = jnp.take(up_adapters, block_owner_tenant, axis=0)
     g_blk = grad.reshape(2, block_list, block_length, head_cols)
     inner_part = jnp.einsum("cbij,bcrj->bicr", g_blk, b_sel, preferred_element_type=jnp.float32)
-    inner = lax.psum(inner_part.reshape(tok_rows, rank_row_slice).astype(jnp.bfloat16), "tensor")
+    inner = jnp.sum(
+        lax.all_gather(inner_part.reshape(tok_rows, rank_row_slice).astype(jnp.bfloat16), "tensor"),
+        axis=0,
+    )
     inner_block = inner.reshape(block_list, block_length, rank_row_slice)
     selected_down = jnp.take(down_adapters, block_owner_tenant, axis=0)
     adapter_input_gradient = jnp.einsum(

time: 340 us -> 209 us (0.61)
  waiting for transfers between devices: 278 us -> 132 us
  blocking collectives: 0 us -> 15.7 us
    reduce_scatter x1, waiting for transfers between devices: 89.8 us -> 0.01 us  [per_device(): lax.psum_scatter(partial_value.astype(jnp.bfloat16), 'tensor', scatter_di...]
    psum x1 -> x0, waiting for transfers between devices: 57.1 us -> none  [per_device(): lax.psum(inner_part.reshape(tok_rows, rank_row_slice).astype(jnp.bfloat16...]
    all_gather x0 -> x1, blocking collectives: none -> 15.7 us  [per_device(): lax.all_gather(inner_part.reshape(tok_rows, rank_row_slice).astype(jnp.bf...]
    unnamed x4 -> x3, waiting for transfers between devices: 131 us -> 132 us
  transfers between devices with their start and end apart: 3 -> 2, of which waited for: 3 -> 1; matrix products, arithmetic and copies ran while one was open for 7% -> 10% of each run, Pallas kernels for 0% -> 0%
where the time goes in v1:
time: 209 us
  waiting for transfers between devices  132 us (63%)
  matrix products  24.5 us (12%)
  between operations  16.9 us (8%)
  blocking collectives  15.7 us (8%)
  local copies, waits for them, and re-layouts  10.3 us (5%)
  other arithmetic  9.79 us (5%)
    unnamed x3, waiting for transfers between devices  132 us
    all_gather x1, blocking collectives, per_device(): lax.all_gather(inner_part.reshape(tok_rows, rank_row_slice).astype(jnp.bf...  15.7 us
    dot_general x1, matrix products, per_device(): jnp.einsum('cnj,cdj->nd', grad, key_value_weight, preferred_element_type=...  10.8 us
    dot_general x1, matrix products, per_device(): jnp.einsum('sb,bcd->scd', onehot, per_block, precision=lax.Precision.HIGH...  9.92 us
    convert_element_type x1, other arithmetic, per_device(): (base_offset + 2.0 * adapter_input_gradient).astype(jnp.bfloat16)  4.96 us
  transfers between devices with their start and end apart: 2, of which 1 were waited for; matrix products, arithmetic and copies ran while one was open for 10% of the time, Pallas kernels for 0%

profile of v1, /device:TPU:1, one launch (start us, length us, event | category | flops | bytes accessed | tf_op | source)
XLA Modules:
  0.0 208.9 jit_solution(17683692758144842754)
XLA Ops:
  8.0 0.0 copy-start
  8.0 0.0 all-reduce.3.cloned.1.call-start
  8.1 0.7 compare_select_fusion
  8.8 0.7 compare_and_fusion
  10.1 0.1 broadcast_bitcast_fusion
  10.2 1.2 broadcast_multiply_fusion
  11.4 0.0 copy-done
  11.5 0.6 gather_fusion
  12.0 0.4 fusion.2
  12.4 0.1 copy.36
  12.5 15.7 %all_gather.4 = bf16[8,1024,32]{1,2,0:T(8,128)(2,1)S(1)} all-gather(bf16[1,1024,32]{1,2,0:T(8,128)(2,1)S(1)} %convert_element_type.51), channel_id=1, replica_groups=mesh['dp'=16,'tensor'=8] {'tensor'}, dimensions={0}, use_global_device_ids=true | all-gather | bytes 589824 | tf_op jit(solution)/shard_map/all_gather | solution.py:34
  28.2 0.8 copy.47
  29.0 0.2 fusion.5
  29.3 0.9 select_reduce_fusion
  30.1 0.1 reduce_sum.21
  30.2 1.8 constant_dynamic-slice_fusion
  32.0 0.4 fusion.9
  32.4 0.1 maximum_multiply_fusion
  32.5 9.9 %convolution_convert_fusion = bf16[128,32,1152]{2,0,1:T(8,128)(2,1)} fusion(f32[8,32,1152]{2,1,0:T(8,128)S(1)} %maximum_multiply_fusion, s32[8]{0:T(128)S(1)} %select_reduce_fusion), kind=kOutput, calls=%fused_computation.3 | convolution fusion | flops 457704448 | bytes 10616864 | tf_op jit(solution)/shard_map/sb,bcd->scd/dot_general | solution.py:68
  42.4 0.0 all-reduce.3.cloned.1.call-update
  42.5 0.0 reduce-scatter.3.cloned.1.call-start
  42.5 10.8 %bitcast_convert_fusion = bf16[1024,8192]{1,0:T(8,128)(2,1)} fusion(bf16[2,1024,128]{2,1,0:T(8,128)(2,1)S(1)} %broadcast_multiply_fusion, bf16[2,8192,128]{2,1,0:T(8,128)(2,1)} %param.11), kind=kOutput, calls=%fused_computation.2 | convolution fusion | flops 4303355904 | bytes 21495808 | tf_op jit(solution)/shard_map/cnj,cdj->nd/dot_general | solution.py:42
  53.3 0.0 copy-start.2
  53.3 0.0 reduce-scatter.3.cloned.1.call-update
  53.3 4.0 %gather_fusion.1 = bf16[8,32,1024]{2,1,0:T(8,128)(2,1)S(1)} fusion(bf16[128,32,1024]{2,1,0:T(8,128)(2,1)} %param.12, s32[1024]{0:T(1024)S(1)} %pad_clamp_fusion), kind=kCustom, calls=%fused_computation.1 | custom fusion | bytes 1048608 | tf_op jit(solution)/shard_map/jit(_take)/gather | solution.py:38
  57.3 0.0 copy-done.2
  57.3 0.6 dynamic-slice
  58.5 2.7 %convolution_multiply_fusion = f32[8,128,1024]{2,1,0:T(8,128)} fusion(bf16[8,32,1024]{2,1,0:T(8,128)(2,1)S(1)} %gather_fusion.1, pred[8]{0:T(512)(128)(4,1)S(1)} %compare_and_fusion, bf16[1024,32]{0,1:T(8,128)(2,1)S(1)} %reduce_sum.21), kind=kOutput, calls=%fused_computation.6 | convolution fusion | flops 68419584 | bytes 4784136 | tf_op jit(solution)/shard_map/hxr,hrg->hxg/dot_general | solution.py:39
  61.3 131.6 %all-reduce.3.cloned.1.call-done = bf16[128,32,1152]{2,0,1:T(8,128)(2,1)} async-done(((bf16[128,32,1152]{2,0,1:T(8,128)(2,1)}), bf16[128,32,1152]{2,0,1:T(8,128)(2,1)}) %all-reduce.3.cloned.1.call-update) | async-done | bytes 9437200
  192.9 1.1 dynamic-slice_convert_fusion
  194.0 0.1 slice.12
  194.2 1.6 copy.42
  195.8 0.0 copy-start.1
  195.8 0.7 copy.43
  196.4 0.0 reduce-scatter.3.cloned.1.call-done
  196.4 5.0 %fusion = bf16[1024,1024]{1,0:T(8,128)(2,1)} fusion(f32[8,128,1024]{2,1,0:T(8,128)} %convolution_multiply_fusion, bf16[1024,1024]{1,0:T(8,128)(2,1)} %reduce-scatter.3.cloned.1.call-done), kind=kLoop, calls=%fused_computation.5 | loop fusion | flops 3145728 | bytes 8388608 | tf_op jit(solution)/shard_map/convert_element_type | solution.py:48
  201.4 0.0 copy-done.1
  (4 shorter events, 0.1 us)
Async XLA Ops:
  8.0 3.5 %copy-start = (bf16[128,2,16,128]{3,2,1,0:T(8,128)(2,1)S(1)}, bf16[128,2,16,128]{3,2,1,0:T(8,128)(2,1)}, u32[]{:S(2)}) copy-start(bf16[128,2,16,128]{3,2,1,0:T(8,128)(2,1)} %param.13) | copy-start | bytes 3145732
  8.0 184.9 %all-reduce.3.cloned.1.call-start = ((), (), s32[]{:S(2)}) async-start(), calls=%async_computation.2 | async-start | bytes 18874368
  42.5 154.0 %reduce-scatter.3.cloned.1.call-start = ((), (), s32[]{:S(2)}) async-start(), calls=%async_computation.1 | async-start | bytes 18874368 | tf_op jit(solution)/shard_map/reduce_scatter | solution.py:45
  53.3 4.0 %copy-start.2 = (u32[128]{0:T(128)S(1)}, u32[128]{0:T(128)}, u32[]{:S(2)}) copy-start(u32[128]{0:T(128)} %constant.47) | copy-start | bytes 1540
  195.8 5.6 %copy-start.1 = (bf16[128,2,16,128]{3,2,1,0:T(8,128)(2,1)S(1)}, bf16[128,2,16,128]{3,2,1,0:T(8,128)(2,1)}, u32[]{:S(2)}) copy-start(bf16[128,2,16,128]{3,2,1,0:T(8,128)(2,1)} %param.13) | copy-start | bytes 3145732
Sparse Core Ops, SparseCore 0:
  42.6 150.2 all-reduce.2
Sparse Core Ops, SparseCore 1:
  53.4 91.9 reduce-scatter.2
